TPU v7x, 512 devices: a whole 4x8x8 slice. The times are simulated.
512 devices in a mesh: ulysses: 8 (over y_lo, core), blk: 64 (over x, z, y_hi).
Axes of the slice: x: 4, y: 8 (y_hi: 2, y_lo: 4; y = y_hi * 4 + y_lo), z: 8, core: 2. Of those that a mesh axis runs over, the one named last changes fastest.
Arguments:
- query_first: bfloat16 [128, 64, 8, 128], P('blk', None, 'ulysses'), may hold values from -6 to 6
- query_second: bfloat16 [128, 64, 8, 128], P('blk', None, 'ulysses'), may hold values from -6 to 6
- key_first: bfloat16 [128, 64, 8, 128], P('blk', None, 'ulysses'), may hold values from -6 to 6
- key_second: bfloat16 [128, 64, 8, 128], P('blk', None, 'ulysses'), may hold values from -6 to 6
- values: bfloat16 [128, 64, 8, 256], P('blk', None, 'ulysses'), may hold values from -6 to 6
- out_first: bfloat16 [128, 64, 8, 256], P('blk', None, 'ulysses'), may hold values from -6 to 6, as said below
- out_second: bfloat16 [128, 64, 8, 256], P('blk', None, 'ulysses'), may hold values from -6 to 6, as said below
- log_totals: float32 [8, 2, 128, 64], P('ulysses', None, 'blk'), as said below
- lambdas: float32 [8], P('ulysses'), may hold values from 0.1 to 0.8
- norm_gain: float32 [8, 256], P('ulysses'), may hold values from 0.1 to 1.9
- cotangent: bfloat16 [128, 64, 8, 256], P('blk', 'ulysses'), may hold values from -6 to 6
- block_of: int32 [128], replicated, may hold values from 0 to 127, as said below
Outputs:
- grad_query_first: bfloat16 [128, 64, 8, 128], P('blk', None, 'ulysses')
- grad_query_second: bfloat16 [128, 64, 8, 128], P('blk', None, 'ulysses')
- grad_key_first: bfloat16 [128, 64, 8, 128], P('blk', None, 'ulysses')
- grad_key_second: bfloat16 [128, 64, 8, 128], P('blk', None, 'ulysses')
- grad_values: bfloat16 [128, 64, 8, 256], P('blk', None, 'ulysses')
Inputs may be any that keep to these rules, and one draw needn't show every extreme that they name: `block_of`: slots 2d and 2d + 1 hold blocks c_d and 127 - c_d, where c_0 to c_last form a permutation of 0 to 63. `out_first`: the causal softmax average of values under the first pair's scaled scores, normalised over visible keys, rounded to bfloat16. `out_second`: likewise for the second pair. log_totals[h, 0] and log_totals[h, 1] are the logarithms of the sums over visible keys of exp of the first and second pair's scaled scores.
All inputs are finite; a program needn't handle non-finite values.
Results may differ from a plain program's by a relative error of at most 0.0085.
Values may be sent and summed in bfloat16 or wider, within the bound.
A program may use at most 64 MiB of HBM per device.

v0:
```python
import math

import jax
import jax.numpy as jnp
from jax import lax
from jax.sharding import PartitionSpec as P

norm_eps = 1e-05


def lookup(block_table, wanted):
    slot_ids = jnp.arange(block_table.shape[0], dtype=jnp.int32)
    return jnp.sum(jnp.where(slot_ids == wanted, block_table, 0))


def shard_positions(block_table, shard_id, block_len):
    lower_block = lookup(block_table, 2 * shard_id)
    upper_block = lookup(block_table, 2 * shard_id + 1)
    offsets = jnp.arange(block_len, dtype=jnp.int32)
    return (
        jnp.concatenate([lower_block * block_len + offsets, upper_block * block_len + offsets]),
        lower_block,
    )


def group_positions(block_table, first_shard, group_size, block_len):
    shard_ids = first_shard + jnp.arange(group_size, dtype=jnp.int32)
    every_pos = jax.vmap(lambda shard_id: shard_positions(block_table, shard_id, block_len)[0])(
        shard_ids
    )
    return every_pos.reshape(-1)


def group_width():
    return 8


def summed(left_terms, right_terms):
    return jax.tree.map(jnp.add, left_terms, right_terms)


def flat_rows(blocked, row_count):
    return blocked.reshape((row_count,) + blocked.shape[2:])


def tile_terms(
    query_part, stats_part, key_part, query_pos, key_pos, lambdas, scale_qk, want_query, want_key
):
    first_query, second_query, grad_out = query_part
    first_key, second_key, values = key_part
    visible = (key_pos[None, :] <= query_pos[:, None])[None]
    score_one = (
        jnp.einsum("qhd,khd->hqk", first_query, first_key, preferred_element_type=jnp.float32)
        * scale_qk
    )
    score_two = (
        jnp.einsum("qhd,khd->hqk", second_query, second_key, preferred_element_type=jnp.float32)
        * scale_qk
    )
    prob_one = jnp.exp(jnp.where(visible, score_one - stats_part[:, 0, :, None], -jnp.inf))
    prob_two = jnp.exp(jnp.where(visible, score_two - stats_part[:, 1, :, None], -jnp.inf))
    grad_attn = jnp.einsum("qhe,khe->hqk", grad_out, values, preferred_element_type=jnp.float32)
    lambda_col = lambdas[:, None, None]
    grad_one = (prob_one * (grad_attn - stats_part[:, 2, :, None])).astype(jnp.bfloat16)
    grad_two = (-lambda_col * prob_two * (grad_attn - stats_part[:, 3, :, None])).astype(
        jnp.bfloat16
    )
    query_terms = None
    key_terms = None
    if want_query:
        query_terms = (
            jnp.einsum("hqk,khd->qhd", grad_one, first_key, preferred_element_type=jnp.float32),
            jnp.einsum("hqk,khd->qhd", grad_two, second_key, preferred_element_type=jnp.float32),
        )
    if want_key:
        weights = (prob_one - lambda_col * prob_two).astype(jnp.bfloat16)
        key_terms = (
            jnp.einsum("hqk,qhd->khd", grad_one, first_query, preferred_element_type=jnp.float32),
            jnp.einsum("hqk,qhd->khd", grad_two, second_query, preferred_element_type=jnp.float32),
            jnp.einsum("hqk,qhe->khe", weights, grad_out, preferred_element_type=jnp.float32),
        )
    return (query_terms, key_terms)


def per_device(
    query_first,
    query_second,
    key_first,
    key_second,
    values,
    out_first,
    out_second,
    log_totals,
    lambdas,
    norm_gain,
    cotangent,
    block_of,
):
    grad_y = lax.all_to_all(cotangent, "ulysses", split_axis=2, concat_axis=1, tiled=True)
    slot_count, block_len, heads_here, value_width = values.shape
    key_width = query_first.shape[3]
    row_count = slot_count * block_len
    scale_qk = 1.0 / math.sqrt(key_width)
    first_out = out_first.astype(jnp.float32)
    second_out = out_second.astype(jnp.float32)
    combined = first_out - lambdas[None, None, :, None] * second_out
    inv_rms = lax.rsqrt(jnp.mean(combined * combined, axis=-1, keepdims=True) + norm_eps)
    gained = norm_gain[None, None] * grad_y.astype(jnp.float32)
    centre = jnp.mean(combined * gained, axis=-1, keepdims=True)
    grad_out = (inv_rms * (gained - combined * inv_rms * inv_rms * centre)).astype(jnp.bfloat16)
    grad_wide = grad_out.astype(jnp.float32)
    dot_one = jnp.sum(grad_wide * first_out, axis=-1).reshape(row_count, heads_here).T
    dot_two = jnp.sum(grad_wide * second_out, axis=-1).reshape(row_count, heads_here).T
    own_stats = jnp.concatenate(
        [log_totals.reshape(heads_here, 2, row_count), dot_one[:, None], dot_two[:, None]], axis=1
    )
    own_query = (
        flat_rows(query_first, row_count),
        flat_rows(query_second, row_count),
        flat_rows(grad_out, row_count),
    )
    own_key = (
        flat_rows(key_first, row_count),
        flat_rows(key_second, row_count),
        flat_rows(values, row_count),
    )
    my_index = lax.axis_index("blk")
    own_pos, own_low = shard_positions(block_of, my_index, block_len)
    query_zero = jnp.zeros((row_count, heads_here, key_width), jnp.float32)
    running = (query_zero, query_zero)
    arrived = (
        lax.all_gather(key_first, "blk", axis=0, tiled=True),
        lax.all_gather(key_second, "blk", axis=0, tiled=True),
        lax.all_gather(values, "blk", axis=0, tiled=True),
    )
    shard_total = arrived[0].shape[0] // 2
    width_now = group_width()
    group_total = shard_total // width_now
    groups = tuple(
        (
            member.reshape((group_total, width_now * row_count) + member.shape[2:])
            for member in arrived
        )
    )

    def one_group(totals, scan_input):
        group_rows, group_step = scan_input
        key_pos = group_positions(block_of, group_step * width_now, width_now, block_len)
        query_new, unused = tile_terms(
            own_query, own_stats, group_rows, own_pos, key_pos, lambdas, scale_qk, True, False
        )
        return (summed(totals, query_new), None)

    running, unused = lax.scan(
        one_group, running, (groups, jnp.arange(group_total, dtype=jnp.int32))
    )
    query_totals = running
    every_stats = lax.all_gather(own_stats, "blk", axis=2, tiled=True)
    value_zero = jnp.zeros((row_count, heads_here, value_width), jnp.float32)
    running = (query_zero, query_zero, value_zero)
    arrived = (
        lax.all_gather(query_first, "blk", axis=0, tiled=True),
        lax.all_gather(query_second, "blk", axis=0, tiled=True),
        lax.all_gather(grad_out, "blk", axis=0, tiled=True),
    )
    shard_total = arrived[0].shape[0] // 2
    fold_width_now = group_width()
    group_total = shard_total // fold_width_now
    groups = tuple(
        (
            member.reshape((group_total, fold_width_now * row_count) + member.shape[2:])
            for member in arrived
        )
    )

    def one_group(totals, scan_input):
        group_rows, group_step = scan_input
        group_first = group_step * fold_width_now
        query_pos = group_positions(block_of, group_first, fold_width_now, block_len)
        group_stats = lax.dynamic_slice_in_dim(
            every_stats, group_first * row_count, fold_width_now * row_count, 2
        )
        unused, key_new = tile_terms(
            group_rows, group_stats, own_key, query_pos, own_pos, lambdas, scale_qk, False, True
        )
        return (summed(totals, key_new), None)

    running, unused = lax.scan(
        one_group, running, (groups, jnp.arange(group_total, dtype=jnp.int32))
    )
    grad_query_first = (query_totals[0] * scale_qk).astype(jnp.bfloat16).reshape(query_first.shape)
    grad_query_second = (query_totals[1] * scale_qk).astype(jnp.bfloat16).reshape(query_first.shape)
    grad_key_first = (running[0] * scale_qk).astype(jnp.bfloat16).reshape(query_first.shape)
    grad_key_second = (running[1] * scale_qk).astype(jnp.bfloat16).reshape(query_first.shape)
    grad_values = running[2].astype(jnp.bfloat16).reshape(values.shape)
    return (grad_query_first, grad_query_second, grad_key_first, grad_key_second, grad_values)


def solution(mesh):
    in_specs = (
        P("blk", None, "ulysses", None),
        P("blk", None, "ulysses", None),
        P("blk", None, "ulysses", None),
        P("blk", None, "ulysses", None),
        P("blk", None, "ulysses", None),
        P("blk", None, "ulysses", None),
        P("blk", None, "ulysses", None),
        P("ulysses", None, "blk", None),
        P("ulysses"),
        P("ulysses", None),
        P("blk", "ulysses", None, None),
        P(),
    )
    out_specs = (
        P("blk", None, "ulysses", None),
        P("blk", None, "ulysses", None),
        P("blk", None, "ulysses", None),
        P("blk", None, "ulysses", None),
        P("blk", None, "ulysses", None),
    )
    return jax.shard_map(
        per_device, mesh=mesh, in_specs=in_specs, out_specs=out_specs, check_vma=False
    )
```

profile of v0, /device:TPU:2, one launch (start us, length us, event | category | flops | bytes accessed | tf_op | source)
XLA Modules:
  0.0 966.0 jit_solution(1171389247158806005)
XLA Ops:
  12.0 4.9 all-to-all-start
  21.1 1.7 all-to-all-done
  23.8 1.6 fusion.99
  25.8 208.0 %all_gather.25 = f32[1,4,8192]{2,1,0:T(4,128)S(1)} all-gather(f32[1,4,128]{2,1,0:T(4,128)S(1)} %pad_maximum_fusion), channel_id=1, replica_groups=mesh['ulysses'=8,'blk'=64] {'blk'}, dimensions={2}, use_global_device_ids=true | all-gather | bytes 133120 | tf_op jit(solution)/shard_map/all_gather | solution.py:158
  233.8 50.9 %all-gather.11.cloned.1.call-done = bf16[128,64,1,128]{3,1,2,0:T(8,128)(2,1)} async-done(((bf16[2,64,1,128]{3,1,2,0:T(8,128)(2,1)}), bf16[128,64,1,128]{3,1,2,0:T(8,128)(2,1)}) %all-gather.11.cloned.1.call-update) | async-done | bytes 2097168 | tf_op jit(solution)/shard_map/all_gather | solution.py:133
  284.8 155.4 %all-gather.9.cloned.1.call-done = bf16[128,64,1,256]{3,1,2,0:T(8,128)(2,1)} async-done(((bf16[2,64,1,256]{3,1,2,0:T(8,128)(2,1)}), bf16[128,64,1,256]{3,1,2,0:T(8,128)(2,1)}) %all-gather.9.cloned.1.call-update) | async-done | bytes 4194320 | tf_op jit(solution)/shard_map/all_gather | solution.py:134
  440.2 54.6 %while.34 = (s32[]{:T(128)}, f32[128,1,128]{0,2,1:T(8,128)S(1)}, f32[128,1,128]{0,2,1:T(8,128)S(1)}, bf16[8,1024,1,128]{3,1,2,0:T(8,128)(2,1)}, s32[8]{0:T(128)S...) while((s32[]{:T(128)}, f32[128,1,128]{0,2,1:T(8,128)S(1)}, ...), condition=%wide.wide.region_9.10_spmd.clone, body=%wide.wide.region_6.9_spmd.clone.sunk | while | flops 203366432 | bytes 3700362 | solution.py:154
  443.9 1.6 fusion.169
  445.5 1.6 fusion.170
  450.8 1.5 fusion.169
  452.4 1.5 fusion.170
  459.2 1.5 fusion.170
  466.0 1.5 fusion.170
  471.3 1.5 fusion.169
  472.8 1.5 fusion.170
  478.1 1.5 fusion.169
  479.6 1.5 fusion.170
  484.9 1.5 fusion.169
  486.4 1.5 fusion.170
  493.2 1.5 fusion.170
  496.3 74.9 %all-gather.13.cloned.1.call-done = bf16[128,64,1,128]{3,1,2,0:T(8,128)(2,1)} async-done(((bf16[2,64,1,128]{3,1,2,0:T(8,128)(2,1)}), bf16[128,64,1,128]{3,1,2,0:T(8,128)(2,1)}) %all-gather.13.cloned.1.call-update) | async-done | bytes 2097168 | tf_op jit(solution)/shard_map/all_gather | solution.py:162
  571.1 133.8 %all-gather.17.cloned.1.call-done = bf16[128,64,1,128]{3,1,2,0:T(8,128)(2,1)} async-done(((bf16[2,64,1,128]{3,1,2,0:T(8,128)(2,1)}), bf16[128,64,1,128]{3,1,2,0:T(8,128)(2,1)}) %all-gather.17.cloned.1.call-update) | async-done | bytes 2097168 | tf_op jit(solution)/shard_map/all_gather | solution.py:163
  705.0 155.8 %all-gather.15.cloned.1.call-done = bf16[128,64,1,256]{3,1,2,0:T(8,128)(2,1)} async-done(((bf16[2,64,1,256]{3,1,2,0:T(8,128)(2,1)}), bf16[128,64,1,256]{3,1,2,0:T(8,128)(2,1)}) %all-gather.15.cloned.1.call-update) | async-done | bytes 4194320 | tf_op jit(solution)/shard_map/all_gather | solution.py:164
  860.8 96.2 %while.33 = (s32[]{:T(128)}, f32[128,1,128]{0,2,1:T(8,128)S(1)}, f32[128,1,128]{0,2,1:T(8,128)S(1)}, f32[128,1,256]{0,2,1:T(8,128)S(1)}, bf16[8,1024,1,128]{3,1,...) while((s32[]{:T(128)}, f32[128,1,128]{0,2,1:T(8,128)S(1)}, ...), condition=%wide.region_13.14_spmd.clone, body=%wide.region_10.13_spmd.clone.sunk | while | flops 270934048 | bytes 7544063 | solution.py:188
  870.7 2.1 fusion.159
  882.7 2.1 fusion.159
  894.8 2.1 fusion.159
  906.8 2.1 fusion.159
  918.8 2.1 fusion.159
  930.8 2.1 fusion.159
  942.9 2.1 fusion.159
  954.9 2.1 fusion.159
  (263 shorter events, 109.5 us)
Async XLA Ops:
  7.2 226.7 %all-gather.7.cloned.1.call-start = ((), (), s32[]{:S(2)}) async-start(), calls=%async_computation.1 | async-start | bytes 2129920 | tf_op jit(solution)/shard_map/all_gather | solution.py:132
  7.9 276.9 %all-gather.11.cloned.1.call-start = ((), (), s32[]{:S(2)}) async-start(), calls=%async_computation.3 | async-start | bytes 2129920 | tf_op jit(solution)/shard_map/all_gather | solution.py:133
  8.6 431.5 %all-gather.9.cloned.1.call-start = ((), (), s32[]{:S(2)}) async-start(), calls=%async_computation.2 | async-start | bytes 4259840 | tf_op jit(solution)/shard_map/all_gather | solution.py:134
  9.4 561.8 %all-gather.13.cloned.1.call-start = ((), (), s32[]{:S(2)}) async-start(), calls=%async_computation.4 | async-start | bytes 2129920 | tf_op jit(solution)/shard_map/all_gather | solution.py:162
  10.0 695.0 %all-gather.17.cloned.1.call-start = ((), (), s32[]{:S(2)}) async-start(), calls=%async_computation.6 | async-start | bytes 2129920 | tf_op jit(solution)/shard_map/all_gather | solution.py:163
  12.0 10.8 %all-to-all-start = ((bf16[2,8,8,256]{3,1,0,2:T(8,128)(2,1)}), bf16[2,8,8,256]{3,1,0,2:T(8,128)(2,1)S(1)}, u32[]{:S(2)}, u32[]{:S(2)}) async-start(bf16[2,8,8,256]{3,1,0,2:T(8,128)(2,1)} %copy.59), calls=%async_computation | async-start | bytes 131072 | tf_op jit(solution)/shard_map/all_to_all | solution.py:99
  16.9 843.8 %all-gather.15.cloned.1.call-start = ((), (), s32[]{:S(2)}) async-start(), calls=%async_computation.5 | async-start | bytes 4259840 | tf_op jit(solution)/shard_map/all_gather | solution.py:164
  25.5 414.7 %copy-start.4 = (f32[2,64]{1,0:T(2,128)}, f32[2,64]{1,0:T(2,128)S(1)}, u32[]{:S(2)}) copy-start(f32[2,64]{1,0:T(2,128)S(1)} %get-tuple-element.590) | copy-start | bytes 1540
  25.5 414.7 %copy-start.5 = (f32[2,64]{1,0:T(2,128)}, f32[2,64]{1,0:T(2,128)S(1)}, u32[]{:S(2)}) copy-start(f32[2,64]{1,0:T(2,128)S(1)} %get-tuple-element.591) | copy-start | bytes 1540
  440.1 420.6 %copy-start = (bf16[2,64,1,256]{3,1,2,0:T(8,128)(2,1)S(1)}, bf16[2,64,1,256]{3,1,2,0:T(8,128)(2,1)}, u32[]{:S(2)}) copy-start(bf16[2,64,1,256]{3,1,2,0:T(8,128)(2,1)} %param.20) | copy-start | bytes 196612
  440.1 420.6 %copy-start.2 = (bf16[2,64,1,128]{3,1,2,0:T(8,128)(2,1)S(1)}, bf16[2,64,1,128]{3,1,2,0:T(8,128)(2,1)}, u32[]{:S(2)}) copy-start(bf16[2,64,1,128]{3,1,2,0:T(8,128)(2,1)} %param.18) | copy-start | bytes 98308
  440.2 420.6 %copy-start.3 = (bf16[2,64,1,128]{3,1,2,0:T(8,128)(2,1)S(1)}, bf16[2,64,1,128]{3,1,2,0:T(8,128)(2,1)}, u32[]{:S(2)}) copy-start(bf16[2,64,1,128]{3,1,2,0:T(8,128)(2,1)} %param.19) | copy-start | bytes 98308
  440.2 5.3 copy-start.1
  447.1 5.3 copy-start.1
  453.9 5.3 copy-start.1
  460.7 5.2 copy-start.1
  467.6 5.3 copy-start.1
  474.4 5.2 copy-start.1
  481.2 5.2 copy-start.1
  488.0 5.2 copy-start.1
Sparse Core Ops, SparseCore 0:
  12.5 141.2 all-gather.6
  158.2 126.5 all-gather.10
  289.1 150.9 all-gather.8
  444.4 126.6 all-gather.12
  575.5 129.4 all-gather.16
  709.8 150.9 all-gather.14
where the time goes:
time: 969 us; the launch traced here: 966 us
  waiting for transfers between devices  576 us (59%)
  blocking collectives  208 us (21%)
  matrix products  106 us (11%)
  other arithmetic  21.8 us (2%)
  loops' own time  16.9 us (2%)
  local copies, waits for them, and re-layouts  16.6 us (2%)
  between operations  16.2 us (2%)
    all_gather x1, blocking collectives, per_device(): every_stats = lax.all_gather(own_stats, 'blk', axis=2, tiled=True)  208 us
    all_gather x1, waiting for transfers between devices, per_device(): lax.all_gather(grad_out, 'blk', axis=0, tiled=True)  156 us
    all_gather x1, waiting for transfers between devices, per_device(): lax.all_gather(values, 'blk', axis=0, tiled=True)  155 us
    all_gather x1, waiting for transfers between devices, per_device(): lax.all_gather(query_second, 'blk', axis=0, tiled=True)  134 us
    all_gather x1, waiting for transfers between devices, per_device(): lax.all_gather(query_first, 'blk', axis=0, tiled=True)  74.9 us
    all_gather x1, waiting for transfers between devices, per_device(): lax.all_gather(key_second, 'blk', axis=0, tiled=True)  50.9 us
    dot_general x16, matrix products, tile_terms(): jnp.einsum('qhe,khe->hqk', grad_out, values, preferred_element_type=jnp.f...  21.4 us
  transfers between devices with their start and end apart: 7, of which 6 were waited for; matrix products, arithmetic and copies ran while one was open for 6% of the time, Pallas kernels for 0%

commit v1 on v0

v1 whole, which is shorter than its diff:
```python
import functools
import math

import jax
import jax.numpy as jnp
from jax import lax
from jax.experimental import pallas as pl
from jax.experimental.pallas import tpu as pltpu
from jax.sharding import PartitionSpec as P

MESH = pl.DeviceIdType.MESH
NX, NZ, NY, NU = 4, 8, 2, 8
ROWS, DH, DV, HALF = 128, 128, 256, 64
GROWS = ROWS + 16
EPS = 1e-05
LOG2E = math.log2(math.e)
F32, BF16 = jnp.float32, jnp.bfloat16
KSLOT = {4: 0, 5: 1, 3: 2, 6: 3, 2: 4, 7: 5, 1: 6, 0: 7}
KFROM = {place: d for d, place in KSLOT.items()}


def qslot(dx, dy):
    return dx + (0 if dy else 4)


def dot(a, b, dims):
    return lax.dot_general(a, b, (dims, ((), ())), preferred_element_type=F32)


def split3(value):
    high = value.astype(BF16)
    rest = value - high.astype(F32)
    middle = rest.astype(BF16)
    low = (rest - middle.astype(F32)).astype(BF16)
    return high.astype(F32), middle.astype(F32), low.astype(F32)


def kernel(
    q1, q2, k1, k2, v, o1, o2, totals, lam_ref, gain, cot, block_of,
    gq1, gq2, gk1, gk2, gv,
    cot_out, cot_in, qb, gb, kb, vb, stat, qpos, gq_sum, gk_sum, gv_sum,
    zs, zr, xs, xr, ys, yr, send, recv,
):
    u = lax.axis_index("ulysses")
    blk = lax.axis_index("blk")
    x, z, y = blk // (NZ * NY), (blk // NY) % NZ, blk % NY

    def at(nx, nz, ny):
        return {"blk": (lax.rem(nx, NX) * NZ + lax.rem(nz, NZ)) * NY + lax.rem(ny, NY)}

    up, down, across = at(x, z + 1, y), at(x, z + NZ - 1, y), at(x, z, y + 1)
    x_peers = {dx: at(x + dx, z, y) for dx in range(1, NX)}
    u_peers = {r: {"ulysses": lax.rem(u + r, NU)} for r in range(1, NU)}
    started = []

    def copy(name, src, dst, device):
        i = names.setdefault(name, len(names))
        return pltpu.make_async_remote_copy(
            src_ref=src, dst_ref=dst, send_sem=send.at[i], recv_sem=recv.at[i],
            device_id=device, device_id_type=MESH,
        )

    names = {}
    moves = {}

    def go(name, src, dst, device):
        move = copy(name, src, dst, device)
        move.start()
        moves[name] = move

    def arrived(name):
        moves[name].wait_recv()

    barrier = pltpu.get_barrier_semaphore()
    partners = [up, down, across, *x_peers.values(), *u_peers.values()]
    for partner in partners:
        pl.semaphore_signal(barrier, inc=1, device_id=partner, device_id_type=MESH)

    own_q, own_k = qslot(0, 0), KSLOT[0]
    qb[own_q, :, :DH] = q1[...]
    qb[own_q, :, DH:] = q2[...]
    kb[own_k, :, :DH] = k1[...]
    kb[own_k, :, DH:] = k2[...]
    vb[own_k] = v[...]
    to_row = lax.broadcasted_iota(jnp.int32, (ROWS, ROWS), 0)
    from_row = lax.broadcasted_iota(jnp.int32, (ROWS, ROWS), 1)
    wanted = (to_row % 16) * 8 + to_row // 16
    order = jnp.where(from_row == wanted, 1.0, 0.0).astype(BF16)
    rows_in = cot[...].astype(F32).reshape(ROWS, DV).astype(BF16)
    by_head = dot(order, rows_in, ((1,), (0,))).astype(BF16).reshape(NU, 16, DV)
    cot_out[...] = by_head

    pl.semaphore_wait(barrier, len(partners))

    for r, device in u_peers.items():
        go(f"c{r}", cot_out.at[lax.rem(u + r, NU)], cot_in.at[u], device)
    for way, device, sign in (("u", up, 1), ("d", down, -1)):
        slot = KSLOT[sign % NZ]
        go(f"k{way}1", kb.at[own_k], kb.at[slot], device)
        go(f"v{way}1", vb.at[own_k], vb.at[slot], device)
    go("qy", qb.at[own_q], qb.at[qslot(0, 1)], across)
    for dx, device in x_peers.items():
        go(f"q{dx}", qb.at[own_q], qb.at[qslot(dx, 0)], device)

    cot_in[u] = cot_out[u]
    for r in u_peers:
        arrived(f"c{r}")
    lam = lam_ref[0]
    parts = cot_in[...].astype(F32)
    grad_y = jnp.concatenate(
        [parts[w, s * 8 : s * 8 + 8] for s in range(2) for w in range(NU)], axis=0
    )
    first_out, second_out = o1[...].astype(F32), o2[...].astype(F32)
    combined = first_out - lam * second_out
    inv_rms = lax.rsqrt(jnp.mean(combined * combined, axis=-1, keepdims=True) + EPS)
    gained = gain[...] * grad_y
    centre = jnp.mean(combined * gained, axis=-1, keepdims=True)
    grad_out = (inv_rms * (gained - combined * inv_rms * inv_rms * centre)).astype(BF16)
    gb[own_q, :ROWS] = grad_out
    wide = grad_out.astype(F32)
    dot_one = jnp.sum(wide * first_out, axis=-1, keepdims=True)
    dot_two = jnp.sum(wide * second_out, axis=-1, keepdims=True)
    row_one = jnp.broadcast_to(dot_one, (ROWS, ROWS)).T[:1]
    row_two = jnp.broadcast_to(dot_two, (ROWS, ROWS)).T[:1]
    log_lam = jnp.log2(jnp.full((1, ROWS), lam, F32))
    total_one = jnp.concatenate([totals[0, 0, :1], totals[0, 0, 1:]], axis=1) * LOG2E
    total_two = jnp.concatenate([totals[0, 1, :1], totals[0, 1, 1:]], axis=1) * LOG2E
    stats = jnp.concatenate([total_one, total_two - log_lam, row_one, row_two], axis=0)
    coded = jnp.concatenate([*split3(stats), jnp.zeros((4, ROWS), F32)], axis=0)
    gb[own_q, ROWS:] = jnp.concatenate([coded, jnp.zeros((16, ROWS), F32)], axis=1).astype(BF16)

    go("gy", gb.at[own_q], gb.at[qslot(0, 1)], across)
    for dx, device in x_peers.items():
        go(f"g{dx}", gb.at[own_q], gb.at[qslot(dx, 0)], device)

    def pass_on(hop, kinds):
        for kind, way, device, sign in kinds:
            arrived(f"{kind}{way}{hop}")
            held = {"k": kb, "v": vb}[kind]
            here, there = KSLOT[sign * hop % NZ], KSLOT[sign * (hop + 1) % NZ]
            go(f"{kind}{way}{hop + 1}", held.at[here], held.at[there], device)

    both = [(kind, way, device, sign) for way, device, sign in (("u", up, 1), ("d", down, -1)) for kind in "kv"]
    pass_on(1, both)
    arrived("qy")
    for dx, device in x_peers.items():
        go(f"p{dx}", qb.at[qslot(0, 1)], qb.at[qslot(dx, 1)], device)
    pass_on(2, both)
    arrived("gy")
    for dx, device in x_peers.items():
        go(f"h{dx}", gb.at[qslot(0, 1)], gb.at[qslot(dx, 1)], device)
    pass_on(3, [both[0], both[3]])
    arrived("vu3")
    arrived("kd3")
    arrived("ku4")
    arrived("vd4")
    for dx in x_peers:
        for name in "qpgh":
            arrived(f"{name}{dx}")

    lane = lax.broadcasted_iota(jnp.int32, (8, ROWS), 1)
    for dy in range(NY):
        for dx in range(NX):
            slot = qslot(dx, dy)
            source = at(x + NX - dx, z, y + dy)["blk"]
            coded = gb[slot, ROWS:, :ROWS].astype(F32)
            c, part = slot // 2, pl.ds(slot % 2 * ROWS, ROWS)
            stat[c, 0:4, part] = coded[0:4] + coded[4:8] + coded[8:12]
            low, high = block_of[2 * source], block_of[2 * source + 1]
            qpos[c, :, part] = jnp.where(lane < HALF, low * HALF + lane, high * HALF + lane - HALF)
    gq_sum[...] = jnp.zeros_like(gq_sum)
    scale = 1.0 / math.sqrt(DH)
    row = lax.broadcasted_iota(jnp.int32, (2 * ROWS, 1), 0)

    def tile(p):
        places = []
        for slot in (2 * p, 2 * p + 1):
            source = at(x, z + NZ - KFROM[slot], y)["blk"]
            places += [block_of[2 * source], block_of[2 * source + 1]]
        start = jnp.where(
            row < ROWS,
            jnp.where(row < HALF, places[0], places[1]),
            jnp.where(row < ROWS + HALF, places[2], places[3]),
        )
        kpos = start * HALF + row % HALF
        gk_sum[p] = jnp.zeros((2 * ROWS, 2 * DH), F32)
        gv_sum[p] = jnp.zeros((2 * ROWS, DV), F32)

        def step(c, carry):
            keys = kb[2 * p : 2 * p + 2].reshape(2 * ROWS, 2 * DH)
            values = vb[2 * p : 2 * p + 2].reshape(2 * ROWS, DV)
            pair = pl.ds(2 * c, 2)
            queries = qb[pair].reshape(2 * ROWS, 2 * DH)
            grads = gb[pair, :ROWS].reshape(2 * ROWS, DV)
            numbers = stat[c]
            seen = kpos <= qpos[c, :1]
            key_one, key_two = keys[:, :DH], keys[:, DH:]
            query_one, query_two = queries[:, :DH], queries[:, DH:]
            far = ((1,), (1,))
            score_one = dot(key_one, query_one, far) * (scale * LOG2E) - numbers[0:1]
            score_two = dot(key_two, query_two, far) * (scale * LOG2E) - numbers[1:2]
            attn = dot(values, grads, far)
            prob_one = jnp.exp2(jnp.where(seen, score_one, -jnp.inf))
            prob_two = jnp.exp2(jnp.where(seen, score_two, -jnp.inf))
            grad_one = (prob_one * (attn - numbers[2:3])).astype(BF16)
            grad_two = (prob_two * (numbers[3:4] - attn)).astype(BF16)
            mix = (prob_one - prob_two).astype(BF16)
            near = ((1,), (0,))
            gk_sum[p, :, :DH] += dot(grad_one, query_one, near)
            gk_sum[p, :, DH:] += dot(grad_two, query_two, near)
            gv_sum[p] += dot(mix, grads, near)
            first = ((0,), (0,))
            gq_sum[pair, :, :DH] += dot(grad_one, key_one, first).reshape(2, ROWS, DH)
            gq_sum[pair, :, DH:] += dot(grad_two, key_two, first).reshape(2, ROWS, DH)
            return carry

        lax.fori_loop(0, 4, step, 0)

    total = {"k": gk_sum, "v": gv_sum}

    def mine(kind, d):
        slot = KSLOT[d % NZ]
        return total[kind][slot // 2, slot % 2 * ROWS : slot % 2 * ROWS + ROWS]

    spot = {"u": 0, "d": 1}

    def place(kind, way, d):
        return {"k": 0, "v": 1}[kind] + 2 * spot[way] + 4 * (d - 1)

    def pass_sum(kind, way, d, joined):
        value = mine(kind, -d if way == "u" else d)
        if joined:
            arrived(f"r{kind}{way}{d + 1}")
            value = value + zr[place(kind, way, d + 1)].astype(F32)
        i = place(kind, way, d)
        zs[i] = value.astype(BF16)
        go(f"r{kind}{way}{d}", zs.at[i], zr.at[i], up if way == "u" else down)

    tile(0)
    pass_sum("k", "u", 4, False)
    pass_sum("v", "d", 4, False)
    pass_sum("v", "u", 3, False)
    tile(1)
    pass_sum("k", "d", 3, False)
    pass_sum("k", "u", 3, True)
    pass_sum("v", "d", 3, True)
    tile(2)
    for way in "ud":
        for kind in "kv":
            pass_sum(kind, way, 2, True)
    tile(3)
    for dx in range(1, NX):
        xs[dx - 1] = gq_sum[qslot(dx, 1)].astype(BF16)
        go(f"s{dx}", xs.at[dx - 1], xr.at[dx - 1], x_peers[NX - dx])
    for dx in range(1, NX):
        xs[dx + 2] = gq_sum[qslot(dx, 0)].astype(BF16)
        go(f"t{dx}", xs.at[dx + 2], xr.at[dx + 2], x_peers[NX - dx])
    for way in "ud":
        for kind in "kv":
            pass_sum(kind, way, 1, True)
    value = gq_sum[qslot(0, 1)]
    for dx in range(1, NX):
        arrived(f"s{dx}")
        value = value + xr[dx - 1].astype(F32)
    ys[...] = value.astype(BF16)
    go("sy", ys, yr, across)
    value = gq_sum[qslot(0, 0)]
    for dx in range(1, NX):
        arrived(f"t{dx}")
        value = value + xr[dx + 2].astype(F32)
    gq_sum[qslot(0, 0)] = value
    for way in "ud":
        for kind in "kv":
            arrived(f"r{kind}{way}1")
    value = mine("k", 0) + zr[place("k", "u", 1)].astype(F32) + zr[place("k", "d", 1)].astype(F32)
    value = value * scale
    gk1[...] = value[:, :DH].astype(BF16)
    gk2[...] = value[:, DH:].astype(BF16)
    value = mine("v", 0) + zr[place("v", "u", 1)].astype(F32) + zr[place("v", "d", 1)].astype(F32)
    gv[...] = value.astype(BF16)
    arrived("sy")
    value = (gq_sum[qslot(0, 0)] + yr[...].astype(F32)) * scale
    gq1[...] = value[:, :DH].astype(BF16)
    gq2[...] = value[:, DH:].astype(BF16)
    for move in moves.values():
        move.wait_send()


def per_device(*arrays):
    q1, q2, k1, k2, v, o1, o2, totals, lam, gain, cot, block_of = arrays
    flat = lambda a: a.reshape(ROWS, a.shape[-1])
    vmem, smem = pl.BlockSpec(memory_space=pltpu.VMEM), pl.BlockSpec(memory_space=pltpu.SMEM)
    copies = 64
    shape = lambda width: jax.ShapeDtypeStruct((ROWS, width), BF16)
    out = pl.pallas_call(
        kernel,
        out_shape=[shape(DH)] * 4 + [shape(DV)],
        in_specs=[vmem] * 8 + [smem, vmem, vmem, smem],
        out_specs=[vmem] * 5,
        scratch_shapes=[
            pltpu.VMEM((NU, 16, DV), BF16),
            pltpu.VMEM((NU, 16, DV), BF16),
            pltpu.VMEM((8, ROWS, 2 * DH), BF16),
            pltpu.VMEM((8, GROWS, DV), BF16),
            pltpu.VMEM((8, ROWS, 2 * DH), BF16),
            pltpu.VMEM((8, ROWS, DV), BF16),
            pltpu.VMEM((4, 8, 2 * ROWS), F32),
            pltpu.VMEM((4, 8, 2 * ROWS), jnp.int32),
            pltpu.VMEM((8, ROWS, 2 * DH), F32),
            pltpu.VMEM((4, 2 * ROWS, 2 * DH), F32),
            pltpu.VMEM((4, 2 * ROWS, DV), F32),
            pltpu.VMEM((16, ROWS, DV), BF16),
            pltpu.VMEM((16, ROWS, DV), BF16),
            pltpu.VMEM((6, ROWS, 2 * DH), BF16),
            pltpu.VMEM((6, ROWS, 2 * DH), BF16),
            pltpu.VMEM((ROWS, 2 * DH), BF16),
            pltpu.VMEM((ROWS, 2 * DH), BF16),
            pltpu.SemaphoreType.DMA((copies,)),
            pltpu.SemaphoreType.DMA((copies,)),
        ],
        compiler_params=pltpu.CompilerParams(
            collective_id=0, has_side_effects=True, vmem_limit_bytes=48 * 1024 * 1024
        ),
    )(
        flat(q1), flat(q2), flat(k1), flat(k2), flat(v), flat(o1), flat(o2),
        totals, lam, gain, cot.reshape(16, NU, DV), block_of,
    )
    return tuple(g.reshape(2, HALF, 1, g.shape[-1]) for g in out)


def solution(mesh):
    rows = P("blk", None, "ulysses", None)
    in_specs = (rows,) * 7 + (
        P("ulysses", None, "blk", None),
        P("ulysses"),
        P("ulysses", None),
        P("blk", "ulysses", None, None),
        P(),
    )
    return jax.shard_map(
        per_device, mesh=mesh, in_specs=in_specs, out_specs=(rows,) * 5, check_vma=False
    )
```

time: 969 us -> 69.3 us (0.07)
  the two profiles are of different devices: /device:TPU:2 before, /device:TPU:56 now
where the time goes in v1:
time: 69.3 us; the launch traced here: 68.7 us
  Pallas kernels  57.2 us (83%)
  local copies, waits for them, and re-layouts  10.1 us (15%)
  between operations  1.33 us (2%)
    pallas_call x1, Pallas kernels, per_device(): pl.pallas_call(kernel, out_shape=[shape(DH)] * 4 + [shape(DV)], in_specs=...  57.2 us
    unnamed x27, local copies, waits for them, and re-layouts  10.1 us

profile of v1, /device:TPU:56, one launch (start us, length us, event | category | flops | bytes accessed | tf_op | source)
XLA Modules:
  0.0 68.7 jit_solution(1614409049996136270)
XLA Ops:
  1.3 0.0 copy-start.8
  1.3 0.0 copy-start.9
  1.3 0.0 copy-start.10
  1.3 0.7 copy-done.8
  2.0 0.0 copy-done.9
  2.0 0.0 copy-done.10
  2.0 0.0 copy-start
  2.0 0.8 %copy-done = bf16[2,64,1,256]{3,1,2,0:T(8,128)(2,1)S(1)} copy-done((bf16[2,64,1,256]{3,1,2,0:T(8,128)(2,1)S(1)}, bf16[2,64,1,256]{3,1,2,0:T(8,128)(2,1)}, u32[]{:S(2)}) %copy-start) | copy-done | bytes 65560
  2.8 0.0 copy-start.1
  2.8 0.8 %copy-done.1 = bf16[2,64,1,256]{3,1,2,0:T(8,128)(2,1)S(1)} copy-done((bf16[2,64,1,256]{3,1,2,0:T(8,128)(2,1)S(1)}, bf16[2,64,1,256]{3,1,2,0:T(8,128)(2,1)}, u32[]{:S(2)}) %copy-start.1) | copy-done | bytes 65560
  3.7 0.0 copy-start.2
  3.7 0.8 %copy-done.2 = bf16[2,64,1,256]{3,1,2,0:T(8,128)(2,1)S(1)} copy-done((bf16[2,64,1,256]{3,1,2,0:T(8,128)(2,1)S(1)}, bf16[2,64,1,256]{3,1,2,0:T(8,128)(2,1)}, u32[]{:S(2)}) %copy-start.2) | copy-done | bytes 65560
  4.5 0.0 copy-start.3
  4.5 0.8 %copy-done.3 = bf16[2,8,8,256]{3,2,1,0:T(8,128)(2,1)S(1)} copy-done((bf16[2,8,8,256]{3,2,1,0:T(8,128)(2,1)S(1)}, bf16[2,8,8,256]{3,2,1,0:T(8,128)(2,1)}, u32[]{:S(2)}) %copy-start.3) | copy-done | bytes 65560
  5.3 0.0 copy-start.4
  5.3 0.8 %copy-done.4 = bf16[2,64,1,128]{3,1,2,0:T(8,128)(2,1)S(1)} copy-done((bf16[2,64,1,128]{3,1,2,0:T(8,128)(2,1)S(1)}, bf16[2,64,1,128]{3,1,2,0:T(8,128)(2,1)}, u32[]{:S(2)}) %copy-start.4) | copy-done | bytes 32792
  6.1 0.0 copy-start.5
  6.1 0.8 %copy-done.5 = bf16[2,64,1,128]{3,1,2,0:T(8,128)(2,1)S(1)} copy-done((bf16[2,64,1,128]{3,1,2,0:T(8,128)(2,1)S(1)}, bf16[2,64,1,128]{3,1,2,0:T(8,128)(2,1)}, u32[]{:S(2)}) %copy-start.5) | copy-done | bytes 32792
  6.9 0.0 copy-start.6
  6.9 0.8 %copy-done.6 = bf16[2,64,1,128]{3,1,2,0:T(8,128)(2,1)S(1)} copy-done((bf16[2,64,1,128]{3,1,2,0:T(8,128)(2,1)S(1)}, bf16[2,64,1,128]{3,1,2,0:T(8,128)(2,1)}, u32[]{:S(2)}) %copy-start.6) | copy-done | bytes 32792
  7.6 0.0 copy-start.7
  7.6 0.8 %copy-done.7 = bf16[2,64,1,128]{3,1,2,0:T(8,128)(2,1)S(1)} copy-done((bf16[2,64,1,128]{3,1,2,0:T(8,128)(2,1)S(1)}, bf16[2,64,1,128]{3,1,2,0:T(8,128)(2,1)}, u32[]{:S(2)}) %copy-start.7) | copy-done | bytes 32792
  8.4 57.2 %shard_map.155 = (bf16[128,128]{1,0:T(8,128)(2,1)S(1)}, bf16[128,128]{1,0:T(8,128)(2,1)S(1)}, bf16[128,128]{1,0:T(8,128)(2,1)S(1)}, bf16[128,128]{1,0:T(8,128)(2,1)S(1)}, bf16[128,256]{1,0:T(8,128)(2,1)S(1)}) custom-call(bf16[128,128]{1,0:T(8,128)(2,1)S(1)} %bitcast.28, bf16[128,128]{1,0:T(8,128)(2,1)S(1)} %bitcast.29, bf16[128,128]{1,0:T(8,128)(2,1)S(1)} %bitcast.30, ...), custom_call_target="tpu_custom_call" | custom-call | tf_op jit(solution)/shard_map/pallas_call | solution.py:295
  65.6 0.6 copy.28
  66.2 0.6 copy.29
  66.8 0.6 copy.30
  67.5 0.6 copy.31
  68.1 0.6 copy.32
Async XLA Ops:
  1.3 0.7 copy-start.8
  1.3 0.7 copy-start.9
  1.3 0.7 copy-start.10
  2.0 0.8 %copy-start = (bf16[2,64,1,256]{3,1,2,0:T(8,128)(2,1)S(1)}, bf16[2,64,1,256]{3,1,2,0:T(8,128)(2,1)}, u32[]{:S(2)}) copy-start(bf16[2,64,1,256]{3,1,2,0:T(8,128)(2,1)} %param.16) | copy-start | bytes 196612
  2.8 0.8 %copy-start.1 = (bf16[2,64,1,256]{3,1,2,0:T(8,128)(2,1)S(1)}, bf16[2,64,1,256]{3,1,2,0:T(8,128)(2,1)}, u32[]{:S(2)}) copy-start(bf16[2,64,1,256]{3,1,2,0:T(8,128)(2,1)} %param.17) | copy-start | bytes 196612
  3.7 0.8 %copy-start.2 = (bf16[2,64,1,256]{3,1,2,0:T(8,128)(2,1)S(1)}, bf16[2,64,1,256]{3,1,2,0:T(8,128)(2,1)}, u32[]{:S(2)}) copy-start(bf16[2,64,1,256]{3,1,2,0:T(8,128)(2,1)} %param.18) | copy-start | bytes 196612
  4.5 0.8 %copy-start.3 = (bf16[2,8,8,256]{3,2,1,0:T(8,128)(2,1)S(1)}, bf16[2,8,8,256]{3,2,1,0:T(8,128)(2,1)}, u32[]{:S(2)}) copy-start(bf16[2,8,8,256]{3,2,1,0:T(8,128)(2,1)} %param.22) | copy-start | bytes 196612
  5.3 0.8 %copy-start.4 = (bf16[2,64,1,128]{3,1,2,0:T(8,128)(2,1)S(1)}, bf16[2,64,1,128]{3,1,2,0:T(8,128)(2,1)}, u32[]{:S(2)}) copy-start(bf16[2,64,1,128]{3,1,2,0:T(8,128)(2,1)} %param.12) | copy-start | bytes 98308
  6.1 0.8 %copy-start.5 = (bf16[2,64,1,128]{3,1,2,0:T(8,128)(2,1)S(1)}, bf16[2,64,1,128]{3,1,2,0:T(8,128)(2,1)}, u32[]{:S(2)}) copy-start(bf16[2,64,1,128]{3,1,2,0:T(8,128)(2,1)} %param.13) | copy-start | bytes 98308
  6.9 0.8 %copy-start.6 = (bf16[2,64,1,128]{3,1,2,0:T(8,128)(2,1)S(1)}, bf16[2,64,1,128]{3,1,2,0:T(8,128)(2,1)}, u32[]{:S(2)}) copy-start(bf16[2,64,1,128]{3,1,2,0:T(8,128)(2,1)} %param.14) | copy-start | bytes 98308
  7.6 0.8 %copy-start.7 = (bf16[2,64,1,128]{3,1,2,0:T(8,128)(2,1)S(1)}, bf16[2,64,1,128]{3,1,2,0:T(8,128)(2,1)}, u32[]{:S(2)}) copy-start(bf16[2,64,1,128]{3,1,2,0:T(8,128)(2,1)} %param.15) | copy-start | bytes 98308

commit v2 on v1

v2 whole, which is shorter than its diff:
```python
import functools
import math

import jax
import jax.numpy as jnp
from jax import lax
from jax.experimental import pallas as pl
from jax.experimental.pallas import tpu as pltpu
from jax.sharding import PartitionSpec as P

MESH = pl.DeviceIdType.MESH
NX, NZ, NY, NU = 4, 8, 2, 8
ROWS, DH, DV, HALF = 128, 128, 256, 64
GROWS = ROWS + 16
EPS = 1e-05
LOG2E = math.log2(math.e)
F32, BF16 = jnp.float32, jnp.bfloat16
KSLOT = {4: 0, 5: 1, 3: 2, 6: 3, 2: 4, 7: 5, 1: 6, 0: 7}
KFROM = {place: d for d, place in KSLOT.items()}


def qslot(dx, dy):
    return dx + (0 if dy else 4)


def dot(a, b, dims):
    return lax.dot_general(a, b, (dims, ((), ())), preferred_element_type=F32)


def split3(value):
    high = value.astype(BF16)
    rest = value - high.astype(F32)
    middle = rest.astype(BF16)
    low = (rest - middle.astype(F32)).astype(BF16)
    return high.astype(F32), middle.astype(F32), low.astype(F32)


def kernel(
    q1, q2, k1, k2, v, o1_in, o2_in, totals_in, lam_ref, gain_in, cot_in_hbm, block_of,
    grads_out,
    o1, o2, totals, gain, cot, local, cot_out, cot_in, qb, gb, kb, vb, stat, qpos, kpos, gq_sum, gk_sum, gv_sum,
    zs, zr, xs, xr, ys, yr, send, recv,
):
    u = lax.axis_index("ulysses")
    blk = lax.axis_index("blk")
    x, z, y = blk // (NZ * NY), (blk // NY) % NZ, blk % NY

    def at(nx, nz, ny):
        return {"blk": (lax.rem(nx, NX) * NZ + lax.rem(nz, NZ)) * NY + lax.rem(ny, NY)}

    up, down, across = at(x, z + 1, y), at(x, z + NZ - 1, y), at(x, z, y + 1)
    x_peers = {dx: at(x + dx, z, y) for dx in range(1, NX)}
    u_peers = {r: {"ulysses": lax.rem(u + r, NU)} for r in range(1, NU)}

    moves = {}

    def view(place):
        return place[0].at[place[1:]] if isinstance(place, tuple) else place

    def move(name):
        i, src, dst, device = moves[name]
        return pltpu.make_async_remote_copy(
            src_ref=view(src), dst_ref=view(dst), send_sem=send.at[i], recv_sem=recv.at[i],
            device_id=device, device_id_type=MESH,
        )

    def go(name, src, dst, device):
        moves[name] = (len(moves), src, dst, device)
        move(name).start()

    def arrived(name):
        move(name).wait_recv()

    own_q, own_k = qslot(0, 0), KSLOT[0]
    loads = []
    for i, (src, dst) in enumerate((
        (cot_in_hbm, cot),
        (k1, kb.at[own_k, :, :DH]), (k2, kb.at[own_k, :, DH:]), (v, vb.at[own_k]),
        (q1, qb.at[own_q, :, :DH]), (q2, qb.at[own_q, :, DH:]),
        (o1_in, o1), (o2_in, o2), (totals_in, totals), (gain_in, gain),
    )):
        load = pltpu.make_async_copy(src, dst, local.at[i])
        load.start()
        loads.append(load)
    first_load, *loads = loads
    barrier = pltpu.get_barrier_semaphore()
    partners = [up, down, across, *x_peers.values(), *u_peers.values()]
    for partner in partners:
        pl.semaphore_signal(barrier, inc=1, device_id=partner, device_id_type=MESH)

    first_load.wait()
    to_row = lax.broadcasted_iota(jnp.int32, (ROWS, ROWS), 0)
    from_row = lax.broadcasted_iota(jnp.int32, (ROWS, ROWS), 1)
    wanted = (to_row % 16) * 8 + to_row // 16
    order = jnp.where(from_row == wanted, 1.0, 0.0).astype(BF16)
    rows_in = cot[...].astype(F32).reshape(ROWS, DV).astype(BF16)
    by_head = dot(order, rows_in, ((1,), (0,))).astype(BF16).reshape(NU, 16, DV)
    cot_out[...] = by_head

    for load in loads:
        load.wait()
    pl.semaphore_wait(barrier, len(partners))

    for r, device in u_peers.items():
        go(f"c{r}", (cot_out, lax.rem(u + r, NU)), (cot_in, u), device)
    for way, device, sign in (("u", up, 1), ("d", down, -1)):
        slot = KSLOT[sign % NZ]
        go(f"k{way}1", (kb, own_k), (kb, slot), device)
        go(f"v{way}1", (vb, own_k), (vb, slot), device)
    go("qy", (qb, own_q), (qb, qslot(0, 1)), across)
    for dx, device in x_peers.items():
        go(f"q{dx}", (qb, own_q), (qb, qslot(dx, 0)), device)

    cot_in[u] = cot_out[u]
    for r in u_peers:
        arrived(f"c{r}")
    lam = lam_ref[0]
    parts = cot_in[...].astype(F32)
    grad_y = jnp.concatenate(
        [parts[w, s * 8 : s * 8 + 8] for s in range(2) for w in range(NU)], axis=0
    )
    first_out, second_out = o1[...].astype(F32), o2[...].astype(F32)
    combined = first_out - lam * second_out
    inv_rms = lax.rsqrt(jnp.mean(combined * combined, axis=-1, keepdims=True) + EPS)
    gained = gain[...] * grad_y
    centre = jnp.mean(combined * gained, axis=-1, keepdims=True)
    grad_out = (inv_rms * (gained - combined * inv_rms * inv_rms * centre)).astype(BF16)
    gb[own_q, :ROWS] = grad_out
    wide = grad_out.astype(F32)
    dot_one = jnp.sum(wide * first_out, axis=-1, keepdims=True)
    dot_two = jnp.sum(wide * second_out, axis=-1, keepdims=True)
    row_one = jnp.broadcast_to(dot_one, (ROWS, ROWS)).T[:1]
    row_two = jnp.broadcast_to(dot_two, (ROWS, ROWS)).T[:1]
    log_lam = jnp.log2(jnp.full((1, ROWS), lam, F32))
    total_one = jnp.concatenate([totals[0, 0, :1], totals[0, 0, 1:]], axis=1) * LOG2E
    total_two = jnp.concatenate([totals[0, 1, :1], totals[0, 1, 1:]], axis=1) * LOG2E
    stats = jnp.concatenate([total_one, total_two - log_lam, row_one, row_two], axis=0)
    coded = jnp.concatenate([*split3(stats), jnp.zeros((4, ROWS), F32)], axis=0)
    gb[own_q, ROWS:] = jnp.concatenate([coded, jnp.zeros((16, ROWS), F32)], axis=1).astype(BF16)

    go("gy", (gb, own_q), (gb, qslot(0, 1)), across)
    for dx, device in x_peers.items():
        go(f"g{dx}", (gb, own_q), (gb, qslot(dx, 0)), device)

    def pass_on(hop, kinds):
        for kind, way, device, sign in kinds:
            arrived(f"{kind}{way}{hop}")
            held = {"k": kb, "v": vb}[kind]
            here, there = KSLOT[sign * hop % NZ], KSLOT[sign * (hop + 1) % NZ]
            go(f"{kind}{way}{hop + 1}", (held, here), (held, there), device)

    both = [(kind, way, device, sign) for way, device, sign in (("u", up, 1), ("d", down, -1)) for kind in "kv"]
    pass_on(1, both)
    arrived("qy")
    for dx, device in x_peers.items():
        go(f"p{dx}", (qb, qslot(0, 1)), (qb, qslot(dx, 1)), device)

    lane = lax.broadcasted_iota(jnp.int32, (8, 4 * HALF), 1)
    for dy in range(NY):
        sources = [at(x + NX - dx, z, y + dy)["blk"] for dx in range(NX)]
        for half in range(2):
            starts = [block_of[2 * source + half] for source in sources]
            start = jnp.where(
                lane < 2 * HALF,
                jnp.where(lane < HALF, starts[0], starts[1]),
                jnp.where(lane < 3 * HALF, starts[2], starts[3]),
            )
            qpos[dy, half] = start * HALF + lane % HALF
    row = lax.broadcasted_iota(jnp.int32, (ROWS, ROWS), 0)
    for slot in range(NZ):
        source = at(x, z + NZ - KFROM[slot], y)["blk"]
        low, high = block_of[2 * source], block_of[2 * source + 1]
        kpos[slot] = jnp.where(row < HALF, low * HALF + row, high * HALF + row - HALF)
    gq_sum[...] = jnp.zeros_like(gq_sum)
    gk_sum[...] = jnp.zeros_like(gk_sum)
    gv_sum[...] = jnp.zeros_like(gv_sum)
    scale = 1.0 / math.sqrt(DH)

    def unpack_stats(dy):
        whole = []
        for dx in range(NX):
            coded = gb[qslot(dx, dy), ROWS:, :ROWS].astype(F32)
            whole.append(coded[0:4] + coded[4:8] + coded[8:12])
        for half in range(2):
            part = slice(half * HALF, half * HALF + HALF)
            for side in range(2):
                pair = [w[:, part] for w in whole[2 * side : 2 * side + 2]]
                stat[dy, half, 0:4, side * ROWS : side * ROWS + ROWS] = jnp.concatenate(pair, axis=1)

    far, near, first = ((1,), (1,)), ((1,), (0,)), ((0,), (0,))

    def scores(keys, values, queries, grads):
        return (
            dot(keys[:, :DH], queries[:, :DH], far),
            dot(keys[:, DH:], queries[:, DH:], far),
            dot(values, grads, far),
        )

    def weights(raw, numbers, places, query_places):
        one, two, attn = raw
        seen = jnp.concatenate([places, places], axis=1) <= query_places
        one = one * (scale * LOG2E) - numbers[0:1]
        two = two * (scale * LOG2E) - numbers[1:2]
        prob_one = jnp.exp2(jnp.where(seen, one, -jnp.inf))
        prob_two = jnp.exp2(jnp.where(seen, two, -jnp.inf))
        grad_one = (prob_one * (attn - numbers[2:3])).astype(BF16)
        grad_two = (prob_two * (numbers[3:4] - attn)).astype(BF16)
        return grad_one, grad_two, (prob_one - prob_two).astype(BF16)

    def tile(i):
        early = i < 4
        dy = jnp.where(early, 0, 1)
        pair = pl.ds(2 * jnp.where(early, 3 - i, i - 4), 2)
        four = pl.ds(jnp.where(early, 4, 0), 4)
        keys = kb[pair].reshape(2 * ROWS, 2 * DH)
        values = vb[pair].reshape(2 * ROWS, DV)
        low_keys = kb[pair, :HALF].reshape(ROWS, 2 * DH)
        low_values = vb[pair, :HALF].reshape(ROWS, DV)
        queries = qb[four, HALF:].reshape(4 * HALF, 2 * DH)
        grads = gb[four, HALF:ROWS].reshape(4 * HALF, DV)
        low_queries = qb[four, :HALF].reshape(4 * HALF, 2 * DH)
        low_grads = gb[four, :HALF].reshape(4 * HALF, DV)
        high_raw = scores(keys, values, queries, grads)
        low_raw = scores(low_keys, low_values, low_queries, low_grads)
        one, two, mix = weights(high_raw, stat[dy, 1], kpos[pair].reshape(2 * ROWS, ROWS), qpos[dy, 1, :1])
        low_one, low_two, low_mix = weights(
            low_raw, stat[dy, 0], kpos[pair, :HALF].reshape(ROWS, ROWS), qpos[dy, 0, :1]
        )
        gq_sum[four, HALF:, :DH] += dot(one, keys[:, :DH], first).reshape(4, HALF, DH)
        gq_sum[four, HALF:, DH:] += dot(two, keys[:, DH:], first).reshape(4, HALF, DH)
        nothing = jnp.zeros((ROWS, DH), BF16)
        apart = jnp.concatenate(
            [
                jnp.concatenate([low_keys[:, :DH], nothing], axis=1),
                jnp.concatenate([nothing, low_keys[:, DH:]], axis=1),
            ],
            axis=0,
        )
        stacked = jnp.concatenate([low_one, low_two], axis=0)
        gq_sum[four, :HALF] += dot(stacked, apart, first).reshape(4, HALF, 2 * DH)
        gk_sum[pair, :, :DH] += dot(one, queries[:, :DH], near).reshape(2, ROWS, DH)
        gk_sum[pair, :, DH:] += dot(two, queries[:, DH:], near).reshape(2, ROWS, DH)
        gv_sum[pair] += dot(mix, grads, near).reshape(2, ROWS, DV)
        gk_sum[pair, :HALF, :DH] += dot(low_one, low_queries[:, :DH], near).reshape(2, HALF, DH)
        gk_sum[pair, :HALF, DH:] += dot(low_two, low_queries[:, DH:], near).reshape(2, HALF, DH)
        gv_sum[pair, :HALF] += dot(low_mix, low_grads, near).reshape(2, HALF, DV)

    total = {"k": gk_sum, "v": gv_sum}

    def mine(kind, d):
        return total[kind][KSLOT[d % NZ]]

    spot = {"u": 0, "d": 1}

    def place(kind, way, d):
        return {"k": 0, "v": 1}[kind] + 2 * spot[way] + 4 * (d - 1)

    def pass_sum(kind, way, d, joined):
        value = mine(kind, -d if way == "u" else d)
        if joined:
            arrived(f"r{kind}{way}{d + 1}")
            value = value + zr[place(kind, way, d + 1)].astype(F32)
        i = place(kind, way, d)
        zs[i] = value.astype(BF16)
        go(f"r{kind}{way}{d}", (zs, i), (zr, i), up if way == "u" else down)

    def send_queries(dy, sends, first_at):
        for dx in range(1, NX):
            xs[dx + first_at] = gq_sum[qslot(dx, dy)].astype(BF16)
            go(f"{sends}{dx}", (xs, dx + first_at), (xr, dx + first_at), x_peers[NX - dx])

    def step(i, carry):
        @pl.when(i == 0)
        def _():
            for dx in x_peers:
                arrived(f"q{dx}")
                arrived(f"g{dx}")
            unpack_stats(0)

        @pl.when(i == 1)
        def _():
            pass_on(2, both)

        @pl.when(i == 2)
        def _():
            arrived("gy")
            for dx, device in x_peers.items():
                go(f"h{dx}", (gb, qslot(0, 1)), (gb, qslot(dx, 1)), device)
            pass_on(3, [both[0], both[3]])
            arrived("vu3")
            arrived("kd3")

        @pl.when(i == 3)
        def _():
            arrived("ku4")
            arrived("vd4")

        @pl.when(i == 4)
        def _():
            send_queries(0, "t", 2)
            for dx in x_peers:
                arrived(f"p{dx}")
                arrived(f"h{dx}")
            unpack_stats(1)

        @pl.when(i == 5)
        def _():
            pass_sum("k", "u", 4, False)
            pass_sum("v", "d", 4, False)
            pass_sum("v", "u", 3, False)

        @pl.when(i == 6)
        def _():
            pass_sum("k", "d", 3, False)

        tile(i)
        return carry

    lax.fori_loop(0, 8, step, 0)
    send_queries(1, "s", -1)
    pass_sum("k", "u", 3, True)
    pass_sum("v", "d", 3, True)
    pass_sum("v", "u", 2, True)
    pass_sum("k", "d", 2, True)
    pass_sum("k", "u", 2, True)
    pass_sum("v", "d", 2, True)
    value = gq_sum[qslot(0, 1)]
    for dx in range(1, NX):
        arrived(f"s{dx}")
        value = value + xr[dx - 1].astype(F32)
    ys[...] = value.astype(BF16)
    go("sy", ys, yr, across)
    pass_sum("v", "u", 1, True)
    pass_sum("k", "d", 1, True)
    pass_sum("k", "u", 1, True)
    pass_sum("v", "d", 1, True)
    value = gq_sum[qslot(0, 0)]
    for dx in range(1, NX):
        arrived(f"t{dx}")
        value = value + xr[dx + 2].astype(F32)
    gq_sum[qslot(0, 0)] = value
    for way in "ud":
        for kind in "kv":
            arrived(f"r{kind}{way}1")
    value = mine("k", 0) + zr[place("k", "u", 1)].astype(F32) + zr[place("k", "d", 1)].astype(F32)
    value = value * scale
    grads_out[1] = value.astype(BF16)
    value = mine("v", 0) + zr[place("v", "u", 1)].astype(F32) + zr[place("v", "d", 1)].astype(F32)
    grads_out[2] = value.astype(BF16)
    arrived("sy")
    value = (gq_sum[qslot(0, 0)] + yr[...].astype(F32)) * scale
    grads_out[0] = value.astype(BF16)
    for name in moves:
        move(name).wait_send()


def finish(grads, gq1, gq2, gk1, gk2, gv, done):
    moves = [
        pltpu.make_async_copy(src, dst, done.at[i])
        for i, (src, dst) in enumerate((
            (grads.at[0, :, :DH], gq1), (grads.at[0, :, DH:], gq2),
            (grads.at[1, :, :DH], gk1), (grads.at[1, :, DH:], gk2), (grads.at[2], gv),
        ))
    ]
    for move in moves:
        move.start()
    for move in moves:
        move.wait()


def per_device(*arrays):
    q1, q2, k1, k2, v, o1, o2, totals, lam, gain, cot, block_of = arrays
    flat = lambda a: a.reshape(ROWS, a.shape[-1])
    hbm = pl.BlockSpec(memory_space=pltpu.HBM)
    vmem, smem = pl.BlockSpec(memory_space=pltpu.VMEM), pl.BlockSpec(memory_space=pltpu.SMEM)
    copies = 64
    shape = lambda width: jax.ShapeDtypeStruct((ROWS, width), BF16)
    grads = pl.pallas_call(
        kernel,
        out_shape=jax.ShapeDtypeStruct((3, ROWS, DV), BF16),
        in_specs=[hbm] * 8 + [smem, hbm, hbm, smem],
        out_specs=vmem,
        scratch_shapes=[
            pltpu.VMEM((ROWS, DV), BF16),
            pltpu.VMEM((ROWS, DV), BF16),
            pltpu.VMEM((1, 2, 2, HALF), F32),
            pltpu.VMEM((1, DV), F32),
            pltpu.VMEM((16, NU, DV), BF16),
            pltpu.SemaphoreType.DMA((10,)),
            pltpu.VMEM((NU, 16, DV), BF16),
            pltpu.VMEM((NU, 16, DV), BF16),
            pltpu.VMEM((8, ROWS, 2 * DH), BF16),
            pltpu.VMEM((8, GROWS, DV), BF16),
            pltpu.VMEM((8, ROWS, 2 * DH), BF16),
            pltpu.VMEM((8, ROWS, DV), BF16),
            pltpu.VMEM((2, 2, 8, 4 * HALF), F32),
            pltpu.VMEM((2, 2, 8, 4 * HALF), jnp.int32),
            pltpu.VMEM((8, ROWS, ROWS), jnp.int32),
            pltpu.VMEM((8, ROWS, 2 * DH), F32),
            pltpu.VMEM((8, ROWS, 2 * DH), F32),
            pltpu.VMEM((8, ROWS, DV), F32),
            pltpu.VMEM((16, ROWS, DV), BF16),
            pltpu.VMEM((16, ROWS, DV), BF16),
            pltpu.VMEM((6, ROWS, 2 * DH), BF16),
            pltpu.VMEM((6, ROWS, 2 * DH), BF16),
            pltpu.VMEM((ROWS, 2 * DH), BF16),
            pltpu.VMEM((ROWS, 2 * DH), BF16),
            pltpu.SemaphoreType.DMA((copies,)),
            pltpu.SemaphoreType.DMA((copies,)),
        ],
        compiler_params=pltpu.CompilerParams(
            collective_id=0, has_side_effects=True, vmem_limit_bytes=56 * 1024 * 1024
        ),
    )(
        flat(q1), flat(q2), flat(k1), flat(k2), flat(v), flat(o1), flat(o2),
        totals, lam, gain, cot.reshape(16, NU, DV), block_of,
    )
    out = pl.pallas_call(
        finish,
        out_shape=[shape(DH)] * 4 + [shape(DV)],
        in_specs=[vmem],
        out_specs=[hbm] * 5,
        scratch_shapes=[pltpu.SemaphoreType.DMA((5,))],
    )(grads)
    return tuple(g.reshape(2, HALF, 1, g.shape[-1]) for g in out)


def solution(mesh):
    rows = P("blk", None, "ulysses", None)
    in_specs = (rows,) * 7 + (
        P("ulysses", None, "blk", None),
        P("ulysses"),
        P("ulysses", None),
        P("blk", "ulysses", None, None),
        P(),
    )
    return jax.shard_map(
        per_device, mesh=mesh, in_specs=in_specs, out_specs=(rows,) * 5, check_vma=False
    )
```

time: 69.3 us -> 56.5 us (0.82)
  the two profiles are of different devices: /device:TPU:56 before, /device:TPU:8 now
where the time goes in v2:
time: 56.5 us; the launch traced here: 56.3 us
  Pallas kernels  55 us (97%)
  between operations  1.29 us (2%)
    pallas_call x1, Pallas kernels, per_device(): pl.pallas_call(kernel, out_shape=jax.ShapeDtypeStruct((3, ROWS, DV), BF16...  53.4 us
    pallas_call x1, Pallas kernels, per_device(): pl.pallas_call(finish, out_shape=[shape(DH)] * 4 + [shape(DV)], in_specs=...  1.64 us

profile of v2, /device:TPU:8, one launch (start us, length us, event | category | flops | bytes accessed | tf_op | source)
XLA Modules:
  0.0 56.3 jit_solution(18400236033911418846)
XLA Ops:
  1.3 53.4 %shard_map.155.grads = bf16[3,128,256]{2,1,0:T(8,128)(2,1)} custom-call(bf16[128,128]{1,0:T(8,128)(2,1)} %bitcast.27, bf16[128,128]{1,0:T(8,128)(2,1)} %bitcast.28, bf16[128,128]{1,0:T(8,128)(2,1)} %bitcast.29, bf16[128,128]{1,0:T(8,128)(2,1)} %bitcast.30, bf16[128,256]{1,0:T(8,128)(2,1)} %bitcast.23, bf16[128,256]{1,0:T(8,128)(2,1)} %bitcast.24, ...), custom_call_target="tpu_custom_call" | custom-call | tf_op jit(solution)/shard_map/pallas_call | solution.py:378
  54.7 1.6 %shard_map.156 = (bf16[128,128]{1,0:T(8,128)(2,1)}, bf16[128,128]{1,0:T(8,128)(2,1)}, bf16[128,128]{1,0:T(8,128)(2,1)}, bf16[128,128]{1,0:T(8,128)(2,1)}, bf16[128,256]{1,0:T(8,128)(2,1)}) custom-call(bf16[3,128,256]{2,1,0:T(8,128)(2,1)} %shard_map.155.grads), custom_call_target="tpu_custom_call" | custom-call | tf_op jit(solution)/shard_map/pallas_call | solution.py:418

commit v3 on v2

--- a/solution.py
+++ b/solution.py
@@ -15,6 +15,8 @@
 EPS = 1e-05
 LOG2E = math.log2(math.e)
 F32, BF16 = jnp.float32, jnp.bfloat16
+PARTS = (slice(0, HALF), slice(HALF, ROWS))
+G_PARTS = (slice(0, HALF), slice(HALF, GROWS))
 KSLOT = {4: 0, 5: 1, 3: 2, 6: 3, 2: 4, 7: 5, 1: 6, 0: 7}
 KFROM = {place: d for d, place in KSLOT.items()}
 
@@ -36,9 +38,9 @@
 
 
 def kernel(
-    q1, q2, k1, k2, v, o1_in, o2_in, totals_in, lam_ref, gain_in, cot_in_hbm, block_of,
+    q1, q2, k1, k2, v, o1_in, o2_in, totals_in, lam_ref, gain_in, cot_in_hbm, block_in,
     grads_out,
-    o1, o2, totals, gain, cot, local, cot_out, cot_in, qb, gb, kb, vb, stat, qpos, kpos, gq_sum, gk_sum, gv_sum,
+    o1, o2, totals, gain, cot, block_of, local, cot_out, cot_in, qb, gb, kb, vb, stat, qpos, kpos, gq_sum, gk_sum, gv_sum,
     zs, zr, xs, xr, ys, yr, send, recv,
 ):
     u = lax.axis_index("ulysses")
@@ -49,7 +51,7 @@
         return {"blk": (lax.rem(nx, NX) * NZ + lax.rem(nz, NZ)) * NY + lax.rem(ny, NY)}
 
     up, down, across = at(x, z + 1, y), at(x, z + NZ - 1, y), at(x, z, y + 1)
-    x_peers = {dx: at(x + dx, z, y) for dx in range(1, NX)}
+    x_peers = {dx: at(x + dx, z, y) for dx in (2, 1, 3)}
     u_peers = {r: {"ulysses": lax.rem(u + r, NU)} for r in range(1, NU)}
 
     moves = {}
@@ -78,6 +80,7 @@
         (k1, kb.at[own_k, :, :DH]), (k2, kb.at[own_k, :, DH:]), (v, vb.at[own_k]),
         (q1, qb.at[own_q, :, :DH]), (q2, qb.at[own_q, :, DH:]),
         (o1_in, o1), (o2_in, o2), (totals_in, totals), (gain_in, gain),
+            (block_in, block_of),
     )):
         load = pltpu.make_async_copy(src, dst, local.at[i])
         load.start()
@@ -99,6 +102,25 @@
 
     for load in loads:
         load.wait()
+    lane = lax.broadcasted_iota(jnp.int32, (8, 4 * HALF), 1)
+    for dy in range(NY):
+        sources = [at(x + NX - dx, z, y + dy)["blk"] for dx in range(NX)]
+        for half in range(2):
+            starts = [block_of[2 * source + half] for source in sources]
+            start = jnp.where(
+                lane < 2 * HALF,
+                jnp.where(lane < HALF, starts[0], starts[1]),
+                jnp.where(lane < 3 * HALF, starts[2], starts[3]),
+            )
+            qpos[dy, half] = start * HALF + lane % HALF
+    row = lax.broadcasted_iota(jnp.int32, (ROWS, ROWS), 0)
+    for slot in range(NZ):
+        source = at(x, z + NZ - KFROM[slot], y)["blk"]
+        low, high = block_of[2 * source], block_of[2 * source + 1]
+        kpos[slot] = jnp.where(row < HALF, low * HALF + row, high * HALF + row - HALF)
+    gq_sum[...] = jnp.zeros_like(gq_sum)
+    gk_sum[...] = jnp.zeros_like(gk_sum)
+    gv_sum[...] = jnp.zeros_like(gv_sum)
     pl.semaphore_wait(barrier, len(partners))
 
     for r, device in u_peers.items():
@@ -106,12 +128,23 @@
     for way, device, sign in (("u", up, 1), ("d", down, -1)):
         slot = KSLOT[sign % NZ]
         go(f"k{way}1", (kb, own_k), (kb, slot), device)
+    for way, device, sign in (("u", up, 1), ("d", down, -1)):
+        slot = KSLOT[sign % NZ]
         go(f"v{way}1", (vb, own_k), (vb, slot), device)
     go("qy", (qb, own_q), (qb, qslot(0, 1)), across)
     for dx, device in x_peers.items():
         go(f"q{dx}", (qb, own_q), (qb, qslot(dx, 0)), device)
 
+    def pass_on(hop, kinds):
+        for kind, way, device, sign in kinds:
+            arrived(f"{kind}{way}{hop}")
+            held = {"k": kb, "v": vb}[kind]
+            here, there = KSLOT[sign * hop % NZ], KSLOT[sign * (hop + 1) % NZ]
+            go(f"{kind}{way}{hop + 1}", (held, here), (held, there), device)
+
+    both = [(kind, way, device, sign) for kind in "kv" for way, device, sign in (("u", up, 1), ("d", down, -1))]
     cot_in[u] = cot_out[u]
+    pass_on(1, both)
     for r in u_peers:
         arrived(f"c{r}")
     lam = lam_ref[0]
@@ -138,42 +171,17 @@
     coded = jnp.concatenate([*split3(stats), jnp.zeros((4, ROWS), F32)], axis=0)
     gb[own_q, ROWS:] = jnp.concatenate([coded, jnp.zeros((16, ROWS), F32)], axis=1).astype(BF16)
 
-    go("gy", (gb, own_q), (gb, qslot(0, 1)), across)
+    for part, rows in enumerate(G_PARTS):
+        go(f"gy{part}", (gb, own_q, rows), (gb, qslot(0, 1), rows), across)
     for dx, device in x_peers.items():
         go(f"g{dx}", (gb, own_q), (gb, qslot(dx, 0)), device)
 
-    def pass_on(hop, kinds):
-        for kind, way, device, sign in kinds:
-            arrived(f"{kind}{way}{hop}")
-            held = {"k": kb, "v": vb}[kind]
-            here, there = KSLOT[sign * hop % NZ], KSLOT[sign * (hop + 1) % NZ]
-            go(f"{kind}{way}{hop + 1}", (held, here), (held, there), device)
-
-    both = [(kind, way, device, sign) for way, device, sign in (("u", up, 1), ("d", down, -1)) for kind in "kv"]
-    pass_on(1, both)
+    pass_on(2, both[:2])
     arrived("qy")
     for dx, device in x_peers.items():
         go(f"p{dx}", (qb, qslot(0, 1)), (qb, qslot(dx, 1)), device)
-
-    lane = lax.broadcasted_iota(jnp.int32, (8, 4 * HALF), 1)
-    for dy in range(NY):
-        sources = [at(x + NX - dx, z, y + dy)["blk"] for dx in range(NX)]
-        for half in range(2):
-            starts = [block_of[2 * source + half] for source in sources]
-            start = jnp.where(
-                lane < 2 * HALF,
-                jnp.where(lane < HALF, starts[0], starts[1]),
-                jnp.where(lane < 3 * HALF, starts[2], starts[3]),
-            )
-            qpos[dy, half] = start * HALF + lane % HALF
-    row = lax.broadcasted_iota(jnp.int32, (ROWS, ROWS), 0)
-    for slot in range(NZ):
-        source = at(x, z + NZ - KFROM[slot], y)["blk"]
-        low, high = block_of[2 * source], block_of[2 * source + 1]
-        kpos[slot] = jnp.where(row < HALF, low * HALF + row, high * HALF + row - HALF)
-    gq_sum[...] = jnp.zeros_like(gq_sum)
-    gk_sum[...] = jnp.zeros_like(gk_sum)
-    gv_sum[...] = jnp.zeros_like(gv_sum)
+    pass_on(2, both[2:])
+
     scale = 1.0 / math.sqrt(DH)
 
     def unpack_stats(dy):
@@ -247,46 +255,53 @@
 
     total = {"k": gk_sum, "v": gv_sum}
 
-    def mine(kind, d):
-        return total[kind][KSLOT[d % NZ]]
-
     spot = {"u": 0, "d": 1}
 
     def place(kind, way, d):
         return {"k": 0, "v": 1}[kind] + 2 * spot[way] + 4 * (d - 1)
 
-    def pass_sum(kind, way, d, joined):
-        value = mine(kind, -d if way == "u" else d)
+    def pass_sum(kind, way, d, joined, part):
+        rows = PARTS[part]
+        value = total[kind][KSLOT[(-d if way == "u" else d) % NZ], rows]
         if joined:
-            arrived(f"r{kind}{way}{d + 1}")
-            value = value + zr[place(kind, way, d + 1)].astype(F32)
+            arrived(f"r{kind}{way}{d + 1}{part}")
+            value = value + zr[place(kind, way, d + 1), rows].astype(F32)
         i = place(kind, way, d)
-        zs[i] = value.astype(BF16)
-        go(f"r{kind}{way}{d}", (zs, i), (zr, i), up if way == "u" else down)
+        zs[i, rows] = value.astype(BF16)
+        go(f"r{kind}{way}{d}{part}", (zs, i, rows), (zr, i, rows), up if way == "u" else down)
+
+    def pass_sums(kinds, d, joined):
+        for part in range(len(PARTS)):
+            for kind, way in zip(kinds, "ud"):
+                if kind in "kv":
+                    pass_sum(kind, way, d, joined, part)
 
     def send_queries(dy, sends, first_at):
-        for dx in range(1, NX):
-            xs[dx + first_at] = gq_sum[qslot(dx, dy)].astype(BF16)
-            go(f"{sends}{dx}", (xs, dx + first_at), (xr, dx + first_at), x_peers[NX - dx])
+        for part, rows in enumerate(PARTS):
+            for dx in (2, 1, 3):
+                i = dx + first_at
+                xs[i, rows] = gq_sum[qslot(dx, dy), rows].astype(BF16)
+                go(f"{sends}{dx}{part}", (xs, i, rows), (xr, i, rows), x_peers[NX - dx])
 
     def step(i, carry):
         @pl.when(i == 0)
         def _():
+            pass_on(3, both[:1])
             for dx in x_peers:
                 arrived(f"q{dx}")
                 arrived(f"g{dx}")
             unpack_stats(0)
+            pass_on(3, both[3:])
 
         @pl.when(i == 1)
         def _():
-            pass_on(2, both)
+            for part, rows in enumerate(G_PARTS):
+                arrived(f"gy{part}")
+                for dx, device in x_peers.items():
+                    go(f"h{dx}{part}", (gb, qslot(0, 1), rows), (gb, qslot(dx, 1), rows), device)
 
         @pl.when(i == 2)
         def _():
-            arrived("gy")
-            for dx, device in x_peers.items():
-                go(f"h{dx}", (gb, qslot(0, 1)), (gb, qslot(dx, 1)), device)
-            pass_on(3, [both[0], both[3]])
             arrived("vu3")
             arrived("kd3")
 
@@ -300,56 +315,56 @@
             send_queries(0, "t", 2)
             for dx in x_peers:
                 arrived(f"p{dx}")
-                arrived(f"h{dx}")
+                for part in range(len(G_PARTS)):
+                    arrived(f"h{dx}{part}")
             unpack_stats(1)
 
         @pl.when(i == 5)
         def _():
-            pass_sum("k", "u", 4, False)
-            pass_sum("v", "d", 4, False)
-            pass_sum("v", "u", 3, False)
+            pass_sums("kv", 4, False)
+            pass_sums("v-", 3, False)
 
         @pl.when(i == 6)
         def _():
-            pass_sum("k", "d", 3, False)
+            pass_sums("-k", 3, False)
 
         tile(i)
         return carry
 
     lax.fori_loop(0, 8, step, 0)
     send_queries(1, "s", -1)
-    pass_sum("k", "u", 3, True)
-    pass_sum("v", "d", 3, True)
-    pass_sum("v", "u", 2, True)
-    pass_sum("k", "d", 2, True)
-    pass_sum("k", "u", 2, True)
-    pass_sum("v", "d", 2, True)
-    value = gq_sum[qslot(0, 1)]
-    for dx in range(1, NX):
-        arrived(f"s{dx}")
-        value = value + xr[dx - 1].astype(F32)
-    ys[...] = value.astype(BF16)
-    go("sy", ys, yr, across)
-    pass_sum("v", "u", 1, True)
-    pass_sum("k", "d", 1, True)
-    pass_sum("k", "u", 1, True)
-    pass_sum("v", "d", 1, True)
-    value = gq_sum[qslot(0, 0)]
-    for dx in range(1, NX):
-        arrived(f"t{dx}")
-        value = value + xr[dx + 2].astype(F32)
-    gq_sum[qslot(0, 0)] = value
-    for way in "ud":
-        for kind in "kv":
-            arrived(f"r{kind}{way}1")
-    value = mine("k", 0) + zr[place("k", "u", 1)].astype(F32) + zr[place("k", "d", 1)].astype(F32)
-    value = value * scale
-    grads_out[1] = value.astype(BF16)
-    value = mine("v", 0) + zr[place("v", "u", 1)].astype(F32) + zr[place("v", "d", 1)].astype(F32)
-    grads_out[2] = value.astype(BF16)
-    arrived("sy")
-    value = (gq_sum[qslot(0, 0)] + yr[...].astype(F32)) * scale
-    grads_out[0] = value.astype(BF16)
+    pass_sums("kv", 3, True)
+    pass_sums("vk", 2, True)
+    for part, rows in enumerate(PARTS):
+        value = gq_sum[qslot(0, 1), rows]
+        for dx in (1, 3, 2):
+            arrived(f"s{dx}{part}")
+            value = value + xr[dx - 1, rows].astype(F32)
+        ys[rows] = value.astype(BF16)
+        go(f"sy{part}", (ys, rows), (yr, rows), across)
+    pass_sums("kv", 2, True)
+    pass_sums("vk", 1, True)
+    for part, rows in enumerate(PARTS):
+        value = gq_sum[qslot(0, 0), rows]
+        for dx in range(1, NX):
+            arrived(f"t{dx}{part}")
+            value = value + xr[dx + 2, rows].astype(F32)
+        gq_sum[qslot(0, 0), rows] = value
+    pass_sums("kv", 1, True)
+    for part, rows in enumerate(PARTS):
+        for kind in "vk":
+            value = total[kind][KSLOT[0], rows]
+            for way in "ud":
+                arrived(f"r{kind}{way}1{part}")
+                value = value + zr[place(kind, way, 1), rows].astype(F32)
+            if kind == "k":
+                grads_out[1, rows] = (value * scale).astype(BF16)
+            else:
+                grads_out[2, rows] = value.astype(BF16)
+    for part, rows in enumerate(PARTS):
+        arrived(f"sy{part}")
+        value = (gq_sum[qslot(0, 0), rows] + yr[rows].astype(F32)) * scale
+        grads_out[0, rows] = value.astype(BF16)
     for name in moves:
         move(name).wait_send()
 
@@ -373,12 +388,12 @@
     flat = lambda a: a.reshape(ROWS, a.shape[-1])
     hbm = pl.BlockSpec(memory_space=pltpu.HBM)
     vmem, smem = pl.BlockSpec(memory_space=pltpu.VMEM), pl.BlockSpec(memory_space=pltpu.SMEM)
-    copies = 64
+    copies = 96
     shape = lambda width: jax.ShapeDtypeStruct((ROWS, width), BF16)
     grads = pl.pallas_call(
         kernel,
-        out_shape=jax.ShapeDtypeStruct((3, ROWS, DV), BF16),
-        in_specs=[hbm] * 8 + [smem, hbm, hbm, smem],
+        out_shape=pltpu.VMEM((3, ROWS, DV), BF16),
+        in_specs=[hbm] * 8 + [smem] + [hbm] * 3,
         out_specs=vmem,
         scratch_shapes=[
             pltpu.VMEM((ROWS, DV), BF16),
@@ -386,7 +401,8 @@
             pltpu.VMEM((1, 2, 2, HALF), F32),
             pltpu.VMEM((1, DV), F32),
             pltpu.VMEM((16, NU, DV), BF16),
-            pltpu.SemaphoreType.DMA((10,)),
+            pltpu.SMEM((128,), jnp.int32),
+            pltpu.SemaphoreType.DMA((11,)),
             pltpu.VMEM((NU, 16, DV), BF16),
             pltpu.VMEM((NU, 16, DV), BF16),
             pltpu.VMEM((8, ROWS, 2 * DH), BF16),
@@ -421,6 +437,7 @@
         in_specs=[vmem],
         out_specs=[hbm] * 5,
         scratch_shapes=[pltpu.SemaphoreType.DMA((5,))],
+        compiler_params=pltpu.CompilerParams(vmem_limit_bytes=4 * 1024 * 1024),
     )(grads)
     return tuple(g.reshape(2, HALF, 1, g.shape[-1]) for g in out)
 

time: 56.5 us -> 53.1 us (0.940)
  Pallas kernels: 55 us -> 51.6 us
    pallas_call x1, Pallas kernels: 53.4 us -> 50.9 us  [per_device(): pl.pallas_call(kernel, out_shape=pltpu.VMEM((3, ROWS, DV), BF16), in_spec...]
    pallas_call x1, Pallas kernels: 1.64 us -> 0.72 us  [per_device(): pl.pallas_call(finish, out_shape=[shape(DH)] * 4 + [shape(DV)], in_specs=...]
where the time goes in v3:
time: 53.1 us; the launch traced here: 52.9 us
  Pallas kernels  51.6 us (97%)
  between operations  1.29 us (2%)
    pallas_call x1, Pallas kernels, per_device(): pl.pallas_call(kernel, out_shape=pltpu.VMEM((3, ROWS, DV), BF16), in_spec...  50.9 us

profile of v3, /device:TPU:8, one launch (start us, length us, event | category | flops | bytes accessed | tf_op | source)
XLA Modules:
  0.0 52.9 jit_solution(9075689941984349134)
XLA Ops:
  1.3 50.9 %shard_map.155.grads = bf16[3,128,256]{2,1,0:T(8,128)(2,1)S(1)} custom-call(bf16[128,128]{1,0:T(8,128)(2,1)} %bitcast.27, bf16[128,128]{1,0:T(8,128)(2,1)} %bitcast.28, bf16[128,128]{1,0:T(8,128)(2,1)} %bitcast.29, bf16[128,128]{1,0:T(8,128)(2,1)} %bitcast.30, bf16[128,256]{1,0:T(8,128)(2,1)} %bitcast.23, bf16[128,256]{1,0:T(8,128)(2,1)} %bitcast.24, ...), custom_call_target="tpu_custom_call" | custom-call | tf_op jit(solution)/shard_map/pallas_call | solution.py:393
  52.2 0.7 %shard_map.156 = (bf16[128,128]{1,0:T(8,128)(2,1)}, bf16[128,128]{1,0:T(8,128)(2,1)}, bf16[128,128]{1,0:T(8,128)(2,1)}, bf16[128,128]{1,0:T(8,128)(2,1)}, bf16[128,256]{1,0:T(8,128)(2,1)}) custom-call(bf16[3,128,256]{2,1,0:T(8,128)(2,1)S(1)} %shard_map.155.grads), custom_call_target="tpu_custom_call" | custom-call | tf_op jit(solution)/shard_map/pallas_call | solution.py:434

commit v4 on v3

--- a/solution.py
+++ b/solution.py
@@ -72,6 +72,14 @@
 
     def arrived(name):
         move(name).wait_recv()
+
+    settled = set()
+
+    def settle(names):
+        for name in names:
+            if name not in settled:
+                move(name).wait_send()
+                settled.add(name)
 
     own_q, own_k = qslot(0, 0), KSLOT[0]
     loads = []
@@ -87,7 +95,7 @@
         loads.append(load)
     first_load, *loads = loads
     barrier = pltpu.get_barrier_semaphore()
-    partners = [up, down, across, *x_peers.values(), *u_peers.values()]
+    partners = [across, *u_peers.values(), *x_peers.values(), up, down]
     for partner in partners:
         pl.semaphore_signal(barrier, inc=1, device_id=partner, device_id_type=MESH)
 
@@ -290,15 +298,12 @@
             for dx in x_peers:
                 arrived(f"q{dx}")
                 arrived(f"g{dx}")
-            unpack_stats(0)
-            pass_on(3, both[3:])
-
-        @pl.when(i == 1)
-        def _():
             for part, rows in enumerate(G_PARTS):
                 arrived(f"gy{part}")
                 for dx, device in x_peers.items():
                     go(f"h{dx}{part}", (gb, qslot(0, 1), rows), (gb, qslot(dx, 1), rows), device)
+            unpack_stats(0)
+            pass_on(3, both[3:])
 
         @pl.when(i == 2)
         def _():
@@ -312,7 +317,6 @@
 
         @pl.when(i == 4)
         def _():
-            send_queries(0, "t", 2)
             for dx in x_peers:
                 arrived(f"p{dx}")
                 for part in range(len(G_PARTS)):
@@ -327,13 +331,17 @@
         @pl.when(i == 6)
         def _():
             pass_sums("-k", 3, False)
+            send_queries(0, "t", 2)
 
         tile(i)
         return carry
 
     lax.fori_loop(0, 8, step, 0)
+    before = list(moves)
     send_queries(1, "s", -1)
+    settle(before[: len(before) // 2])
     pass_sums("kv", 3, True)
+    settle(before)
     pass_sums("vk", 2, True)
     for part, rows in enumerate(PARTS):
         value = gq_sum[qslot(0, 1), rows]
@@ -361,12 +369,11 @@
                 grads_out[1, rows] = (value * scale).astype(BF16)
             else:
                 grads_out[2, rows] = value.astype(BF16)
+    settle(list(moves))
     for part, rows in enumerate(PARTS):
         arrived(f"sy{part}")
         value = (gq_sum[qslot(0, 0), rows] + yr[rows].astype(F32)) * scale
         grads_out[0, rows] = value.astype(BF16)
-    for name in moves:
-        move(name).wait_send()
 
 
 def finish(grads, gq1, gq2, gk1, gk2, gv, done):

time: 53.1 us -> 50.9 us (0.959)
  Pallas kernels: 51.6 us -> 49.4 us
    pallas_call x1, Pallas kernels: 50.9 us -> 48.7 us  [per_device(): pl.pallas_call(kernel, out_shape=pltpu.VMEM((3, ROWS, DV), BF16), in_spec...]
where the time goes in v4:
time: 50.9 us; the launch traced here: 50.7 us
  Pallas kernels  49.4 us (97%)
  between operations  1.29 us (3%)
    pallas_call x1, Pallas kernels, per_device(): pl.pallas_call(kernel, out_shape=pltpu.VMEM((3, ROWS, DV), BF16), in_spec...  48.7 us

profile of v4, /device:TPU:8, one launch (start us, length us, event | category | flops | bytes accessed | tf_op | source)
XLA Modules:
  0.0 50.7 jit_solution(10146928217103588800)
XLA Ops:
  1.3 48.7 %shard_map.155.grads = bf16[3,128,256]{2,1,0:T(8,128)(2,1)S(1)} custom-call(bf16[128,128]{1,0:T(8,128)(2,1)} %bitcast.27, bf16[128,128]{1,0:T(8,128)(2,1)} %bitcast.28, bf16[128,128]{1,0:T(8,128)(2,1)} %bitcast.29, bf16[128,128]{1,0:T(8,128)(2,1)} %bitcast.30, bf16[128,256]{1,0:T(8,128)(2,1)} %bitcast.23, bf16[128,256]{1,0:T(8,128)(2,1)} %bitcast.24, ...), custom_call_target="tpu_custom_call" | custom-call | tf_op jit(solution)/shard_map/pallas_call | solution.py:400
  50.0 0.7 %shard_map.156 = (bf16[128,128]{1,0:T(8,128)(2,1)}, bf16[128,128]{1,0:T(8,128)(2,1)}, bf16[128,128]{1,0:T(8,128)(2,1)}, bf16[128,128]{1,0:T(8,128)(2,1)}, bf16[128,256]{1,0:T(8,128)(2,1)}) custom-call(bf16[3,128,256]{2,1,0:T(8,128)(2,1)S(1)} %shard_map.155.grads), custom_call_target="tpu_custom_call" | custom-call | tf_op jit(solution)/shard_map/pallas_call | solution.py:441

commit v5 on v4

--- a/solution.py
+++ b/solution.py
@@ -110,6 +110,20 @@
 
     for load in loads:
         load.wait()
+    pl.semaphore_wait(barrier, len(partners))
+
+    for r, device in u_peers.items():
+        go(f"c{r}", (cot_out, lax.rem(u + r, NU)), (cot_in, u), device)
+    for way, device, sign in (("u", up, 1), ("d", down, -1)):
+        slot = KSLOT[sign % NZ]
+        go(f"k{way}1", (kb, own_k), (kb, slot), device)
+    for way, device, sign in (("u", up, 1), ("d", down, -1)):
+        slot = KSLOT[sign % NZ]
+        go(f"v{way}1", (vb, own_k), (vb, slot), device)
+    go("qy", (qb, own_q), (qb, qslot(0, 1)), across)
+    for dx, device in x_peers.items():
+        go(f"q{dx}", (qb, own_q), (qb, qslot(dx, 0)), device)
+
     lane = lax.broadcasted_iota(jnp.int32, (8, 4 * HALF), 1)
     for dy in range(NY):
         sources = [at(x + NX - dx, z, y + dy)["blk"] for dx in range(NX)]
@@ -129,20 +143,6 @@
     gq_sum[...] = jnp.zeros_like(gq_sum)
     gk_sum[...] = jnp.zeros_like(gk_sum)
     gv_sum[...] = jnp.zeros_like(gv_sum)
-    pl.semaphore_wait(barrier, len(partners))
-
-    for r, device in u_peers.items():
-        go(f"c{r}", (cot_out, lax.rem(u + r, NU)), (cot_in, u), device)
-    for way, device, sign in (("u", up, 1), ("d", down, -1)):
-        slot = KSLOT[sign % NZ]
-        go(f"k{way}1", (kb, own_k), (kb, slot), device)
-    for way, device, sign in (("u", up, 1), ("d", down, -1)):
-        slot = KSLOT[sign % NZ]
-        go(f"v{way}1", (vb, own_k), (vb, slot), device)
-    go("qy", (qb, own_q), (qb, qslot(0, 1)), across)
-    for dx, device in x_peers.items():
-        go(f"q{dx}", (qb, own_q), (qb, qslot(dx, 0)), device)
-
     def pass_on(hop, kinds):
         for kind, way, device, sign in kinds:
             arrived(f"{kind}{way}{hop}")
@@ -331,7 +331,6 @@
         @pl.when(i == 6)
         def _():
             pass_sums("-k", 3, False)
-            send_queries(0, "t", 2)
 
         tile(i)
         return carry
@@ -341,6 +340,7 @@
     send_queries(1, "s", -1)
     settle(before[: len(before) // 2])
     pass_sums("kv", 3, True)
+    send_queries(0, "t", 2)
     settle(before)
     pass_sums("vk", 2, True)
     for part, rows in enumerate(PARTS):

time: 50.9 us -> 50.9 us (level)
  no operation moved by 1% of the time
where the time goes in v5:
time: 50.9 us; the launch traced here: 50.6 us
  Pallas kernels  49.3 us (97%)
  between operations  1.29 us (3%)
    pallas_call x1, Pallas kernels, per_device(): pl.pallas_call(kernel, out_shape=pltpu.VMEM((3, ROWS, DV), BF16), in_spec...  48.6 us

profile of v5, /device:TPU:8, one launch (start us, length us, event | category | flops | bytes accessed | tf_op | source)
XLA Modules:
  0.0 50.6 jit_solution(2546694972529553436)
XLA Ops:
  1.3 48.6 %shard_map.155.grads = bf16[3,128,256]{2,1,0:T(8,128)(2,1)S(1)} custom-call(bf16[128,128]{1,0:T(8,128)(2,1)} %bitcast.27, bf16[128,128]{1,0:T(8,128)(2,1)} %bitcast.28, bf16[128,128]{1,0:T(8,128)(2,1)} %bitcast.29, bf16[128,128]{1,0:T(8,128)(2,1)} %bitcast.30, bf16[128,256]{1,0:T(8,128)(2,1)} %bitcast.23, bf16[128,256]{1,0:T(8,128)(2,1)} %bitcast.24, ...), custom_call_target="tpu_custom_call" | custom-call | tf_op jit(solution)/shard_map/pallas_call | solution.py:400
  49.8 0.7 %shard_map.156 = (bf16[128,128]{1,0:T(8,128)(2,1)}, bf16[128,128]{1,0:T(8,128)(2,1)}, bf16[128,128]{1,0:T(8,128)(2,1)}, bf16[128,128]{1,0:T(8,128)(2,1)}, bf16[128,256]{1,0:T(8,128)(2,1)}) custom-call(bf16[3,128,256]{2,1,0:T(8,128)(2,1)S(1)} %shard_map.155.grads), custom_call_target="tpu_custom_call" | custom-call | tf_op jit(solution)/shard_map/pallas_call | solution.py:441
